TPU v7x, 256 devices: a whole 4x4x8 slice. The times are simulated.
256 devices in a mesh: ctx: 16 (over z, x_hi), head: 4 (over x_lo, core), doc: 4 (over y).
Axes of the slice: x: 4 (x_hi: 2, x_lo: 2; x = x_hi * 2 + x_lo), y: 4, z: 8, core: 2. Of those that a mesh axis runs over, the one named last changes fastest.
Arguments:
- queries: bfloat16 [16384, 8192], P(('doc', 'ctx'), 'head'), parts along dimension 0, may hold values from -80 to 80
- keys: bfloat16 [16384, 1024], P(('doc', 'ctx'), 'head'), parts along dimension 0, may hold values from -4 to 4
- values: bfloat16 [16384, 1024], P(('doc', 'ctx'), 'head'), parts along dimension 0, may hold values from -6 to 6
- image_keys: bfloat16 [32768, 1024], P(('doc', 'ctx'), 'head'), parts along dimension 0, may hold values from -24 to 24
- image_values: bfloat16 [32768, 1024], P(('doc', 'ctx'), 'head'), parts along dimension 0, may hold values from -6 to 6
- cross_lo: int32 [16384], P(('doc', 'ctx')), parts along dimension 0, may hold values from 0 to 4096, as said below
- cross_hi: int32 [16384], P(('doc', 'ctx')), parts along dimension 0, may hold values from 0 to 8192, as said below
- query_gain: float32 [128], replicated, may hold values from 0.5 to 2
- cross_gate: float32 [64], P('head'), may hold values from -1.5 to 1.5
Outputs:
- self_heads: bfloat16 [16384, 8192], P(('doc', 'ctx'), 'head'), parts along dimension 0
- cross_heads: bfloat16 [16384, 8192], P(('doc', 'ctx'), 'head'), parts along dimension 0
There are 4 independent parts, one for each index of `doc`. A program takes and returns all parts, laid end to end along the dimension named above; an argument that names none is the same for every part. Nothing has to cross between parts.
Inputs may be any that keep to these rules, and one draw needn't show every extreme that they name: `cross_lo`: images sit at distinct token positions after the first token. A token's range covers whole images of 2048 tokens: it ends after the last image placed at or before the token and begins at most two images before that end; tokens before the first image have an empty range. cross_hi[t] >= cross_lo[t], a multiple of 2048, never falling along the document.
All inputs are finite; a program needn't handle non-finite values.
Results may differ from a plain program's by a relative error of at most 0.018.
Values may be sent and summed in bfloat16 or wider, within the bound.
A program may use at most 64 MiB of HBM per device.

v0:
```python
import math

import jax
import jax.numpy as jnp
from jax import lax
from jax.sharding import PartitionSpec as P

HD = 128


NEG = -1e30
EPS = 1e-05


def attend_tile(state_held, query_split, key_tile, value_tile, allowed):
    peak_old, total_old, mixed_old = state_held
    scores = jnp.einsum(
        "tcgd,scd->cgts", query_split, key_tile, preferred_element_type=jnp.float32
    ) * (1.0 / math.sqrt(HD))
    scores = jnp.where(allowed, scores, NEG)
    peak_new = jnp.maximum(peak_old, jnp.max(scores, axis=-1))
    weights = jnp.where(allowed, jnp.exp(scores - peak_new[..., None]), 0.0)
    factor = jnp.exp(peak_old - peak_new)
    total_new = total_old * factor + jnp.sum(weights, axis=-1)
    mixed_new = mixed_old * factor[..., None] + jnp.einsum(
        "cgts,scd->cgtd",
        weights.astype(jnp.bfloat16),
        value_tile,
        preferred_element_type=jnp.float32,
    )
    return (peak_new, total_new, mixed_new)


def make_fold(query_split, allowed_fn, state_held, pieces):
    key_piece, value_piece = pieces
    piece_rows = key_piece.shape[0]
    tile_rows = math.gcd(piece_rows, 512)
    tiles = piece_rows // tile_rows
    kv_local = key_piece.shape[1] // HD
    key_tiles = key_piece.reshape(tiles, tile_rows, kv_local, HD)
    value_tiles = value_piece.reshape(tiles, tile_rows, kv_local, HD)

    def tile_step(carried, inputs):
        key_tile, value_tile, tile_index = inputs
        allowed = allowed_fn(tile_index * tile_rows, tile_rows)
        carried = lax.cond(
            jnp.any(allowed),
            lambda state_in: attend_tile(state_in, query_split, key_tile, value_tile, allowed),
            lambda state_in: state_in,
            carried,
        )
        return (carried, None)

    return lax.scan(
        tile_step, state_held, (key_tiles, value_tiles, jnp.arange(tiles, dtype=jnp.int32))
    )[0]


def empty_state(kv_local, groups, tok_rows):
    shape_rows = (kv_local, groups, tok_rows)
    return (
        jnp.full(shape_rows, NEG, jnp.float32),
        jnp.zeros(shape_rows, jnp.float32),
        jnp.zeros(shape_rows + (HD,), jnp.float32),
    )


def by_tokens(
    queries, keys, values, image_keys, image_values, cross_lo, cross_hi, query_gain, cross_gate
):
    tok_rows = queries.shape[0]
    my_index = lax.axis_index("ctx")
    local_rows = jnp.arange(tok_rows, dtype=jnp.int32)
    query_used, key_used, value_used = (queries, keys, values)
    query_pos = my_index * tok_rows + local_rows

    def key_positions(first_row, tile_rows):
        return first_row + jnp.arange(tile_rows, dtype=jnp.int32)

    def causal(first_row, tile_rows):
        return key_positions(first_row, tile_rows)[None, :] <= query_pos[:, None]

    kv_local = key_used.shape[1] // HD
    groups = query_used.shape[1] // HD // kv_local
    query_split = query_used.reshape(tok_rows, kv_local, groups, HD)
    self_peak, self_total, self_mixed = make_fold(
        query_split,
        causal,
        empty_state(kv_local, groups, tok_rows),
        (
            lax.all_gather(key_used, "ctx", axis=0, tiled=True),
            lax.all_gather(value_used, "ctx", axis=0, tiled=True),
        ),
    )
    self_local = (
        (self_mixed / self_total[..., None])
        .transpose(2, 0, 1, 3)
        .reshape(tok_rows, -1)
        .astype(jnp.bfloat16)
    )
    heads_wide = self_local.astype(jnp.float32).reshape(tok_rows, -1, HD)
    scaling = lax.rsqrt(jnp.mean(heads_wide * heads_wide, axis=-1, keepdims=True) + EPS)
    cross_split = (
        (heads_wide * scaling * query_gain)
        .astype(jnp.bfloat16)
        .reshape(tok_rows, kv_local, groups, HD)
    )

    def ranged(first_row, tile_rows):
        image_index = first_row + jnp.arange(tile_rows, dtype=jnp.int32)
        return (image_index[None, :] >= cross_lo[:, None]) & (
            image_index[None, :] < cross_hi[:, None]
        )

    cross_peak, cross_total, cross_mixed = make_fold(
        cross_split,
        ranged,
        empty_state(kv_local, groups, tok_rows),
        (
            lax.all_gather(image_keys, "ctx", axis=0, tiled=True),
            lax.all_gather(image_values, "ctx", axis=0, tiled=True),
        ),
    )
    attended = (
        (cross_mixed / jnp.maximum(cross_total, 1.0)[..., None])
        .transpose(2, 0, 1, 3)
        .reshape(tok_rows, -1, HD)
    )
    has_image = (cross_hi > cross_lo)[:, None, None]
    gated = jnp.where(has_image, attended * jnp.tanh(cross_gate)[None, :, None], 0.0)
    return (self_local, gated.reshape(tok_rows, -1).astype(jnp.bfloat16))


def per_device(
    queries, keys, values, image_keys, image_values, cross_lo, cross_hi, query_gain, cross_gate
):
    return by_tokens(
        queries, keys, values, image_keys, image_values, cross_lo, cross_hi, query_gain, cross_gate
    )


def solution(mesh):
    placed = (
        P(("doc", "ctx"), "head"),
        P(("doc", "ctx"), "head"),
        P(("doc", "ctx"), "head"),
        P(("doc", "ctx"), "head"),
        P(("doc", "ctx"), "head"),
        P(("doc", "ctx")),
        P(("doc", "ctx")),
        P(),
        P("head"),
    )
    return jax.shard_map(
        per_device,
        mesh=mesh,
        in_specs=placed,
        out_specs=(P(("doc", "ctx"), "head"), P(("doc", "ctx"), "head")),
        check_vma=False,
    )
```

profile of v0, /device:TPU:118, one launch (start us, length us, event | category | flops | bytes accessed | tf_op | source)
XLA Modules:
  0.0 551.5 jit_solution(10023760596390215040)
XLA Ops:
  12.3 83.4 %all-gather.5.cloned.1.call-done = bf16[4096,256]{1,0:T(8,128)(2,1)} async-done(((bf16[256,256]{1,0:T(8,128)(2,1)}), bf16[4096,256]{1,0:T(8,128)(2,1)}) %all-gather.5.cloned.1.call-update) | async-done | bytes 2097168 | tf_op jit(solution)/shard_map/all_gather | solution.py:91
  100.0 80.5 %all-gather.7.cloned.1.call-done = bf16[4096,256]{1,0:T(8,128)(2,1)} async-done(((bf16[256,256]{1,0:T(8,128)(2,1)}), bf16[4096,256]{1,0:T(8,128)(2,1)}) %all-gather.7.cloned.1.call-update) | async-done | bytes 2097168 | tf_op jit(solution)/shard_map/all_gather | solution.py:92
  185.1 56.6 %while.30 = (s32[]{:T(128)}, f32[2,8,256]{2,1,0:T(8,128)S(1)}, f32[2,8,256]{2,1,0:T(8,128)S(1)}, f32[2,8,256,128]{3,2,1,0:T(8,128)S(1)}, s32[8]{0:T(128)S(1)}, /...) while((s32[]{:T(128)}, f32[2,8,256]{2,1,0:T(8,128)S(1)}, ...), condition=%wide.region_6.7_spmd.clone, body=%wide.region_0.6_spmd.clone.sunk | while | flops 1102324480 | bytes 31726860 | solution.py:54
  187.8 8.8 %conditional.6 = ((f32[2,8,256]{2,1,0:T(8,128)S(1)}, f32[2,8,256]{2,1,0:T(8,128)S(1)}, f32[2,8,256,128]{3,2,1,0:T(8,128)S(1)})) conditional(s32[]{:T(128)} %convert_element_type.75, (f32[2,8,256]{2,1,0:T(8,128)S(1)}, f32[2,8,256]{2,1,0:T(8,128)S(1)}, f32[2,8,256,128]{3,2,1,0:T(8,128)S(1)}) %tuple.81, (pred[256,512]{0,1:T(8,128)(4,1)S(1)}, ...), branch_computations={%region_2.2_spmd, %region_3.5_spmd} | conditional | flops 1102061568 | bytes 31589408 | solution.py:46
  199.2 8.8 %conditional.6 = ((f32[2,8,256]{2,1,0:T(8,128)S(1)}, f32[2,8,256]{2,1,0:T(8,128)S(1)}, f32[2,8,256,128]{3,2,1,0:T(8,128)S(1)})) conditional(s32[]{:T(128)} %convert_element_type.75, (f32[2,8,256]{2,1,0:T(8,128)S(1)}, f32[2,8,256]{2,1,0:T(8,128)S(1)}, f32[2,8,256,128]{3,2,1,0:T(8,128)S(1)}) %tuple.81, (pred[256,512]{0,1:T(8,128)(4,1)S(1)}, ...), branch_computations={%region_2.2_spmd, %region_3.5_spmd} | conditional | flops 1102061568 | bytes 31589408 | solution.py:46
  203.6 4.4 multiply_add_fusion
  210.7 8.8 %conditional.6 = ((f32[2,8,256]{2,1,0:T(8,128)S(1)}, f32[2,8,256]{2,1,0:T(8,128)S(1)}, f32[2,8,256,128]{3,2,1,0:T(8,128)S(1)})) conditional(s32[]{:T(128)} %convert_element_type.75, (f32[2,8,256]{2,1,0:T(8,128)S(1)}, f32[2,8,256]{2,1,0:T(8,128)S(1)}, f32[2,8,256,128]{3,2,1,0:T(8,128)S(1)}) %tuple.81, (pred[256,512]{0,1:T(8,128)(4,1)S(1)}, ...), branch_computations={%region_2.2_spmd, %region_3.5_spmd} | conditional | flops 1102061568 | bytes 31589408 | solution.py:46
  215.0 4.4 multiply_add_fusion
  222.1 8.8 %conditional.6 = ((f32[2,8,256]{2,1,0:T(8,128)S(1)}, f32[2,8,256]{2,1,0:T(8,128)S(1)}, f32[2,8,256,128]{3,2,1,0:T(8,128)S(1)})) conditional(s32[]{:T(128)} %convert_element_type.75, (f32[2,8,256]{2,1,0:T(8,128)S(1)}, f32[2,8,256]{2,1,0:T(8,128)S(1)}, f32[2,8,256,128]{3,2,1,0:T(8,128)S(1)}) %tuple.81, (pred[256,512]{0,1:T(8,128)(4,1)S(1)}, ...), branch_computations={%region_2.2_spmd, %region_3.5_spmd} | conditional | flops 1102061568 | bytes 31589408 | solution.py:46
  226.5 4.4 multiply_add_fusion
  245.7 34.1 %all-gather.9.cloned.1.call-done = bf16[8192,256]{1,0:T(8,128)(2,1)} async-done(((bf16[512,256]{1,0:T(8,128)(2,1)}), bf16[8192,256]{1,0:T(8,128)(2,1)}) %all-gather.9.cloned.1.call-update) | async-done | bytes 4194320 | tf_op jit(solution)/shard_map/all_gather | solution.py:120
  279.7 6.9 %reshape.79 = bf16[16,512,2,128]{3,2,1,0:T(2,128)(2,1)} reshape(bf16[8192,256]{1,0:T(8,128)(2,1)} %all-gather.9.cloned.1.call-done) | data formatting | bytes 8388608 | tf_op jit(solution)/shard_map/reshape | solution.py:40
  286.6 5.2 copy.26
  291.8 86.8 %all-gather.11.cloned.1.call-done = bf16[8192,256]{1,0:T(8,128)(2,1)} async-done(((bf16[512,256]{1,0:T(8,128)(2,1)}), bf16[8192,256]{1,0:T(8,128)(2,1)}) %all-gather.11.cloned.1.call-update) | async-done | bytes 4194320 | tf_op jit(solution)/shard_map/all_gather | solution.py:121
  378.6 6.9 %reshape.80 = bf16[16,512,2,128]{3,2,1,0:T(2,128)(2,1)} reshape(bf16[8192,256]{1,0:T(8,128)(2,1)} %all-gather.11.cloned.1.call-done) | data formatting | bytes 8388608 | tf_op jit(solution)/shard_map/reshape | solution.py:41
  385.5 5.1 copy.27
  390.9 150.3 %while.29 = (s32[]{:T(128)}, f32[2,8,256]{2,1,0:T(8,128)S(1)}, f32[2,8,256]{2,1,0:T(8,128)S(1)}, f32[2,8,256,128]{3,2,1,0:T(8,128)S(1)}, s32[16]{0:T(128)S(1)}, ...) while((s32[]{:T(128)}, f32[2,8,256]{2,1,0:T(8,128)S(1)}, ...), condition=%wide.region_14.15_spmd, body=%wide.region_8.14_spmd.sunk | while | flops 1102586368 | bytes 31726864 | solution.py:54
  393.9 8.8 %conditional.5 = ((f32[2,8,256]{2,1,0:T(8,128)S(1)}, f32[2,8,256]{2,1,0:T(8,128)S(1)}, f32[2,8,256,128]{3,2,1,0:T(8,128)S(1)})) conditional(s32[]{:T(128)} %convert_element_type.74, (f32[2,8,256]{2,1,0:T(8,128)S(1)}, f32[2,8,256]{2,1,0:T(8,128)S(1)}, f32[2,8,256,128]{3,2,1,0:T(8,128)S(1)}) %tuple.77, (pred[256,512]{0,1:T(8,128)(4,1)S(1)}, ...), branch_computations={%region_10.10_spmd, %region_11.13_spmd} | conditional | flops 1102061568 | bytes 31589408 | solution.py:46
  398.3 4.4 multiply_add_fusion.2
  405.5 8.8 %conditional.5 = ((f32[2,8,256]{2,1,0:T(8,128)S(1)}, f32[2,8,256]{2,1,0:T(8,128)S(1)}, f32[2,8,256,128]{3,2,1,0:T(8,128)S(1)})) conditional(s32[]{:T(128)} %convert_element_type.74, (f32[2,8,256]{2,1,0:T(8,128)S(1)}, f32[2,8,256]{2,1,0:T(8,128)S(1)}, f32[2,8,256,128]{3,2,1,0:T(8,128)S(1)}) %tuple.77, (pred[256,512]{0,1:T(8,128)(4,1)S(1)}, ...), branch_computations={%region_10.10_spmd, %region_11.13_spmd} | conditional | flops 1102061568 | bytes 31589408 | solution.py:46
  409.8 4.4 multiply_add_fusion.2
  417.0 8.8 %conditional.5 = ((f32[2,8,256]{2,1,0:T(8,128)S(1)}, f32[2,8,256]{2,1,0:T(8,128)S(1)}, f32[2,8,256,128]{3,2,1,0:T(8,128)S(1)})) conditional(s32[]{:T(128)} %convert_element_type.74, (f32[2,8,256]{2,1,0:T(8,128)S(1)}, f32[2,8,256]{2,1,0:T(8,128)S(1)}, f32[2,8,256,128]{3,2,1,0:T(8,128)S(1)}) %tuple.77, (pred[256,512]{0,1:T(8,128)(4,1)S(1)}, ...), branch_computations={%region_10.10_spmd, %region_11.13_spmd} | conditional | flops 1102061568 | bytes 31589408 | solution.py:46
  428.6 8.8 %conditional.5 = ((f32[2,8,256]{2,1,0:T(8,128)S(1)}, f32[2,8,256]{2,1,0:T(8,128)S(1)}, f32[2,8,256,128]{3,2,1,0:T(8,128)S(1)})) conditional(s32[]{:T(128)} %convert_element_type.74, (f32[2,8,256]{2,1,0:T(8,128)S(1)}, f32[2,8,256]{2,1,0:T(8,128)S(1)}, f32[2,8,256,128]{3,2,1,0:T(8,128)S(1)}) %tuple.77, (pred[256,512]{0,1:T(8,128)(4,1)S(1)}, ...), branch_computations={%region_10.10_spmd, %region_11.13_spmd} | conditional | flops 1102061568 | bytes 31589408 | solution.py:46
  433.0 4.4 multiply_add_fusion.2
  440.2 8.8 %conditional.5 = ((f32[2,8,256]{2,1,0:T(8,128)S(1)}, f32[2,8,256]{2,1,0:T(8,128)S(1)}, f32[2,8,256,128]{3,2,1,0:T(8,128)S(1)})) conditional(s32[]{:T(128)} %convert_element_type.74, (f32[2,8,256]{2,1,0:T(8,128)S(1)}, f32[2,8,256]{2,1,0:T(8,128)S(1)}, f32[2,8,256,128]{3,2,1,0:T(8,128)S(1)}) %tuple.77, (pred[256,512]{0,1:T(8,128)(4,1)S(1)}, ...), branch_computations={%region_10.10_spmd, %region_11.13_spmd} | conditional | flops 1102061568 | bytes 31589408 | solution.py:46
  451.7 8.8 %conditional.5 = ((f32[2,8,256]{2,1,0:T(8,128)S(1)}, f32[2,8,256]{2,1,0:T(8,128)S(1)}, f32[2,8,256,128]{3,2,1,0:T(8,128)S(1)})) conditional(s32[]{:T(128)} %convert_element_type.74, (f32[2,8,256]{2,1,0:T(8,128)S(1)}, f32[2,8,256]{2,1,0:T(8,128)S(1)}, f32[2,8,256,128]{3,2,1,0:T(8,128)S(1)}) %tuple.77, (pred[256,512]{0,1:T(8,128)(4,1)S(1)}, ...), branch_computations={%region_10.10_spmd, %region_11.13_spmd} | conditional | flops 1102061568 | bytes 31589408 | solution.py:46
  463.3 8.8 %conditional.5 = ((f32[2,8,256]{2,1,0:T(8,128)S(1)}, f32[2,8,256]{2,1,0:T(8,128)S(1)}, f32[2,8,256,128]{3,2,1,0:T(8,128)S(1)})) conditional(s32[]{:T(128)} %convert_element_type.74, (f32[2,8,256]{2,1,0:T(8,128)S(1)}, f32[2,8,256]{2,1,0:T(8,128)S(1)}, f32[2,8,256,128]{3,2,1,0:T(8,128)S(1)}) %tuple.77, (pred[256,512]{0,1:T(8,128)(4,1)S(1)}, ...), branch_computations={%region_10.10_spmd, %region_11.13_spmd} | conditional | flops 1102061568 | bytes 31589408 | solution.py:46
  474.9 8.8 %conditional.5 = ((f32[2,8,256]{2,1,0:T(8,128)S(1)}, f32[2,8,256]{2,1,0:T(8,128)S(1)}, f32[2,8,256,128]{3,2,1,0:T(8,128)S(1)})) conditional(s32[]{:T(128)} %convert_element_type.74, (f32[2,8,256]{2,1,0:T(8,128)S(1)}, f32[2,8,256]{2,1,0:T(8,128)S(1)}, f32[2,8,256,128]{3,2,1,0:T(8,128)S(1)}) %tuple.77, (pred[256,512]{0,1:T(8,128)(4,1)S(1)}, ...), branch_computations={%region_10.10_spmd, %region_11.13_spmd} | conditional | flops 1102061568 | bytes 31589408 | solution.py:46
  486.5 8.8 %conditional.5 = ((f32[2,8,256]{2,1,0:T(8,128)S(1)}, f32[2,8,256]{2,1,0:T(8,128)S(1)}, f32[2,8,256,128]{3,2,1,0:T(8,128)S(1)})) conditional(s32[]{:T(128)} %convert_element_type.74, (f32[2,8,256]{2,1,0:T(8,128)S(1)}, f32[2,8,256]{2,1,0:T(8,128)S(1)}, f32[2,8,256,128]{3,2,1,0:T(8,128)S(1)}) %tuple.77, (pred[256,512]{0,1:T(8,128)(4,1)S(1)}, ...), branch_computations={%region_10.10_spmd, %region_11.13_spmd} | conditional | flops 1102061568 | bytes 31589408 | solution.py:46
  498.0 8.8 %conditional.5 = ((f32[2,8,256]{2,1,0:T(8,128)S(1)}, f32[2,8,256]{2,1,0:T(8,128)S(1)}, f32[2,8,256,128]{3,2,1,0:T(8,128)S(1)})) conditional(s32[]{:T(128)} %convert_element_type.74, (f32[2,8,256]{2,1,0:T(8,128)S(1)}, f32[2,8,256]{2,1,0:T(8,128)S(1)}, f32[2,8,256,128]{3,2,1,0:T(8,128)S(1)}) %tuple.77, (pred[256,512]{0,1:T(8,128)(4,1)S(1)}, ...), branch_computations={%region_10.10_spmd, %region_11.13_spmd} | conditional | flops 1102061568 | bytes 31589408 | solution.py:46
  509.6 8.8 %conditional.5 = ((f32[2,8,256]{2,1,0:T(8,128)S(1)}, f32[2,8,256]{2,1,0:T(8,128)S(1)}, f32[2,8,256,128]{3,2,1,0:T(8,128)S(1)})) conditional(s32[]{:T(128)} %convert_element_type.74, (f32[2,8,256]{2,1,0:T(8,128)S(1)}, f32[2,8,256]{2,1,0:T(8,128)S(1)}, f32[2,8,256,128]{3,2,1,0:T(8,128)S(1)}) %tuple.77, (pred[256,512]{0,1:T(8,128)(4,1)S(1)}, ...), branch_computations={%region_10.10_spmd, %region_11.13_spmd} | conditional | flops 1102061568 | bytes 31589408 | solution.py:46
  521.2 8.8 %conditional.5 = ((f32[2,8,256]{2,1,0:T(8,128)S(1)}, f32[2,8,256]{2,1,0:T(8,128)S(1)}, f32[2,8,256,128]{3,2,1,0:T(8,128)S(1)})) conditional(s32[]{:T(128)} %convert_element_type.74, (f32[2,8,256]{2,1,0:T(8,128)S(1)}, f32[2,8,256]{2,1,0:T(8,128)S(1)}, f32[2,8,256,128]{3,2,1,0:T(8,128)S(1)}) %tuple.77, (pred[256,512]{0,1:T(8,128)(4,1)S(1)}, ...), branch_computations={%region_10.10_spmd, %region_11.13_spmd} | conditional | flops 1102061568 | bytes 31589408 | solution.py:46
  (220 shorter events, 170.4 us)
Async XLA Ops:
  7.2 5.0 copy-start.3
  7.2 5.0 copy-start
  7.2 5.0 copy-start.1
  7.2 88.5 %all-gather.5.cloned.1.call-start = ((), (), s32[]{:S(2)}) async-start(), calls=%async_computation | async-start | bytes 2228224 | tf_op jit(solution)/shard_map/all_gather | solution.py:91
  7.9 172.6 %all-gather.7.cloned.1.call-start = ((), (), s32[]{:S(2)}) async-start(), calls=%async_computation.1 | async-start | bytes 2228224 | tf_op jit(solution)/shard_map/all_gather | solution.py:92
  8.7 271.0 %all-gather.9.cloned.1.call-start = ((), (), s32[]{:S(2)}) async-start(), calls=%async_computation.2 | async-start | bytes 4456448 | tf_op jit(solution)/shard_map/all_gather | solution.py:120
  9.4 369.2 %all-gather.11.cloned.1.call-start = ((), (), s32[]{:S(2)}) async-start(), calls=%async_computation.3 | async-start | bytes 4456448 | tf_op jit(solution)/shard_map/all_gather | solution.py:121
  241.7 3.3 copy-start.2
Sparse Core Ops, SparseCore 0:
  10.6 85.0 all-gather.4
  98.3 82.2 all-gather.6
  183.2 96.5 all-gather.8
  282.2 96.3 all-gather.10
where the time goes:
time: 554 us; the launch traced here: 551 us
  waiting for transfers between devices  287 us (52%)
  matrix products  107 us (19%)
  other arithmetic  57.4 us (10%)
  local copies, waits for them, and re-layouts  53.6 us (10%)
  loops' own time  32 us (6%)
  between operations  14 us (3%)
    all_gather x1, waiting for transfers between devices, by_tokens(): lax.all_gather(image_values, 'ctx', axis=0, tiled=True)  86.8 us
    all_gather x1, waiting for transfers between devices, by_tokens(): lax.all_gather(key_used, 'ctx', axis=0, tiled=True)  83.4 us
    all_gather x1, waiting for transfers between devices, by_tokens(): lax.all_gather(value_used, 'ctx', axis=0, tiled=True)  80.5 us
    dot_general x16, matrix products, attend_tile(): jnp.einsum('cgts,scd->cgtd', weights.astype(jnp.bfloat16), value_tile, pr...  69.8 us
    dot_general x16, matrix products, attend_tile(): jnp.einsum('tcgd,scd->cgts', query_split, key_tile, preferred_element_typ...  37.1 us
    all_gather x1, waiting for transfers between devices, by_tokens(): lax.all_gather(image_keys, 'ctx', axis=0, tiled=True)  34.1 us
    reduce_sum x16, other arithmetic, attend_tile(): total_new = total_old * factor + jnp.sum(weights, axis=-1)  32.1 us
    another operation x2, loops' own time, make_fold(): lax.scan(tile_step, state_held, (key_tiles, value_tiles, jnp.arange(tiles...  31 us
  transfers between devices with their start and end apart: 4, of which 4 were waited for; matrix products, arithmetic and copies ran while one was open for 13% of the time, Pallas kernels for 0%

commit v1 on v0

v1 whole, which is shorter than its diff:
```python
import math

import jax
import jax.numpy as jnp
from jax import lax
from jax.experimental import pallas as pl
from jax.experimental.pallas import tpu as pltpu
from jax.sharding import PartitionSpec as P

HD = 128
IMG = 2048
EPS = 1e-05
NEG = -1e30
LEVELS = 8
HEADS = 8
LAST = 6
MESH = pl.DeviceIdType.MESH
SCALE = 1.4426950408889634 / math.sqrt(HD)


def dot_nt(a, b):
    return lax.dot_general(a, b, (((1,), (1,)), ((), ())), preferred_element_type=jnp.float32)


def dot_nn(a, b):
    return lax.dot_general(a, b, (((1,), (0,)), ((), ())), preferred_element_type=jnp.float32)


def split_scaled(x):
    x = x * SCALE
    high = x.astype(jnp.bfloat16)
    low = (x - high.astype(jnp.float32)).astype(jnp.bfloat16)
    return high, low


def kernel(
    q_ref, k_ref, v_ref, ik_ref, iv_ref, allow_ref, gain_ref, gate_ref,
    self_ref, cross_ref,
    kv, st_self, st_img, q_in, allow_in, split_q, peak, mixed, allowed,
    st_so, st_co, so_in, co_in, keys2, values1,
    z_send, z_recv, x_send, x_recv,
):
    me = lax.axis_index("ctx")
    z, half = me // 2, me % 2
    rows = q_ref.shape[0]
    img_rows = ik_ref.shape[0]
    wide = HEADS * HD
    partner = {"ctx": z * 2 + (1 - half)}
    up = {"ctx": lax.rem(z + 1, LEVELS) * 2 + half}
    down = {"ctx": lax.rem(z + LEVELS - 1, LEVELS) * 2 + half}

    barrier = pltpu.get_barrier_semaphore()
    for other in (partner, up, down):
        pl.semaphore_signal(barrier, inc=1, device_id=other, device_id_type=MESH)

    own_col = pl.ds(pl.multiple_of(half * HD, HD), HD)
    other_col = pl.ds(pl.multiple_of((1 - half) * HD, HD), HD)
    own_wide = pl.ds(pl.multiple_of(half * wide, wide), wide)
    other_wide = pl.ds(pl.multiple_of((1 - half) * wide, wide), wide)

    def part(kind, level, h):
        if kind == 0:
            start = lax.rem(level, 2) * 2 * rows + h * rows
            return kv.at[level // 2, pl.ds(pl.multiple_of(start, rows), rows), :]
        start = h * img_rows
        return kv.at[LEVELS // 2 + level, pl.ds(pl.multiple_of(start, img_rows), img_rows), :]

    for kind, stage, key_ref, value_ref in (
        (0, st_self, k_ref, v_ref),
        (1, st_img, ik_ref, iv_ref),
    ):
        mine = part(kind, z, half)
        mine[:, :HD] = key_ref[:, own_col]
        mine[:, HD:] = value_ref[:, own_col]
        stage[:, :HD] = key_ref[:, other_col]
        stage[:, HD:] = value_ref[:, other_col]

    def x_copy(slot, src, dst):
        return pltpu.make_async_remote_copy(
            src_ref=src, dst_ref=dst, send_sem=x_send.at[slot], recv_sem=x_recv.at[slot],
            device_id=partner, device_id_type=MESH,
        )

    x_self = x_copy(0, st_self, part(0, z, half))
    x_query = x_copy(1, q_ref.at[:, other_wide], q_in)
    x_allow = x_copy(2, allow_ref, allow_in)
    x_img = x_copy(3, st_img, part(1, z, half))
    x_so = x_copy(4, st_so, so_in)

    def x_co(pair):
        cols = pl.ds(pair * 2 * HD, 2 * HD)
        return x_copy(5 + pair, st_co.at[1, :, cols], co_in.at[:, cols])

    def z_copy(kind, d, n, level, h):
        return pltpu.make_async_remote_copy(
            src_ref=part(kind, level, h), dst_ref=part(kind, level, h),
            send_sem=z_send.at[kind, d, n], recv_sem=z_recv.at[kind, d, n],
            device_id=(up, down)[d], device_id_type=MESH,
        )

    def half_of(d, n):
        if n == LAST:
            return (half, 1 - half)[d]
        return (half, 1 - half)[n % 2]

    def outgoing(kind, d, n):
        level = (z + LEVELS - n // 2, z + n // 2)[d]
        return z_copy(kind, d, n, lax.rem(level, LEVELS), half_of(d, n))

    def incoming(kind, d, n):
        level = (z + LEVELS - 1 - n // 2, z + 1 + n // 2)[d]
        return z_copy(kind, d, n, lax.rem(level, LEVELS), half_of(d, n))

    got = set()

    def await_in(kind, d, n):
        if (kind, d, n) not in got:
            got.add((kind, d, n))
            incoming(kind, d, n).wait_recv()

    def forward(kind, n, ways=(0, 1)):
        for d in ways:
            if n >= 2:
                await_in(kind, d, 5 if (n == LAST and d == 1) else n - 2)
            outgoing(kind, d, n).start()

    def query_rows(slot, h, x):
        high, low = split_scaled(x)
        split_q[slot, h, :, :HD] = high
        split_q[slot, h, :, HD:] = low

    def prepare(slot, read):
        def one(h, _):
            cols = pl.ds(pl.multiple_of(h * HD, HD), HD)
            query_rows(slot, h, read(cols).astype(jnp.float32))
            return 0
        lax.fori_loop(0, HEADS, one, 0)

    def load(piece):
        keys = kv[piece, :, :HD]
        keys2[:, :HD] = keys
        keys2[:, HD:] = keys
        values1[:, :HD] = kv[piece, :, HD:]

    def scores_of(tile, mask=None):
        scores = dot_nt(split_q[tile], keys2[...])
        return scores if mask is None else jnp.where(mask(tile[0], scores.shape), scores, NEG)

    def fold(scores, state, seen=None):
        top = jnp.max(scores, axis=1, keepdims=True)
        if seen is not None:
            top = jnp.where(seen, top, NEG)
        if state is not None:
            top = jnp.maximum(state[0], top)
        shift = top if seen is None else jnp.where(seen, top, -NEG)
        weights = jnp.exp2(scores - shift).astype(jnp.bfloat16)
        term = dot_nn(weights, values1[...])
        if state is not None:
            term = state[1] * jnp.exp2(state[0] - top) + term
        return top, term

    def held(tile):
        return peak[tile][:, :1], mixed[tile]

    def keep(tile, state):
        peak[tile] = jnp.broadcast_to(state[0], peak.shape[2:])
        mixed[tile] = state[1]

    def seen_by(slot, group):
        return allowed[slot, group][:, :1] > 0.5

    def own_order(slot):
        return lax.rem(half + slot, 2)

    def attend(tiles, first=False, mask=None, group=None):
        following = scores_of(tiles[0], mask)
        views = {}
        for n, tile in enumerate(tiles):
            scores = following
            if n + 1 < len(tiles):
                following = scores_of(tiles[n + 1], mask)
            if group is not None and id(tile[0]) not in views:
                views[id(tile[0])] = seen_by(tile[0], group)
            seen = views.get(id(tile[0]))
            keep(tile, fold(scores, None if first else held(tile), seen))

    both = [(s, h) for h in range(HEADS) for s in (0, 1)]

    def causal(slot, shape):
        at_row = z * 2 * rows + own_order(slot) * rows
        at_key = (z // 2) * 4 * rows
        row = at_row - at_key + lax.broadcasted_iota(jnp.int32, shape, 0)
        return lax.broadcasted_iota(jnp.int32, shape, 1) <= row

    values1[:, HD:] = jnp.ones((4 * rows, HD), jnp.bfloat16)

    pl.semaphore_wait(barrier, 3)
    x_self.start()
    forward(0, 0)
    prepare(0, lambda cols: q_ref[:, pl.ds(pl.multiple_of(half * wide + cols.start, HD), HD)])
    x_self.wait_recv()
    x_query.start()
    forward(0, 1)
    forward(0, 2)
    forward(0, 3)

    early = jnp.where(lax.rem(z, 2) == 1, 0, 2)

    def begin(slot, _):
        @pl.when(slot == 1)
        def _():
            x_query.wait_recv()
            x_allow.start()
            x_img.start()
            prepare(1, lambda cols: q_in[:, cols])

        tiles = [(slot, h) for h in range(HEADS)]
        load(z // 2)
        attend(tiles, True, causal)

        @pl.when(slot == 0)
        def _():
            forward(0, 4)
            forward(0, 5)

        @pl.when(z >= 6)
        def _():
            load(early)
            attend(tiles)

        @pl.when(slot == 0)
        def _():
            forward(0, 6)
            forward(1, 0)
        return 0

    lax.fori_loop(0, 2, begin, 0)
    x_img.wait_recv()
    forward(1, 1)
    for d in (0, 1):
        for n in (4, 5, 6):
            await_in(0, d, n)
    x_allow.wait_recv()
    for slot, ref in ((0, allow_ref), (1, allow_in)):
        for image in range(4):
            allowed[slot, image] = jnp.broadcast_to(
                ref[:, image:image + 1].astype(jnp.float32), allowed.shape[2:]
            )
        allowed[slot, 4] = jnp.ones(allowed.shape[2:], jnp.float32)

    def finish_self(h, _):
        cols = pl.ds(pl.multiple_of(h * HD, HD), HD)
        for slot in (1, 0):
            acc = mixed[slot, h]
            out = (acc[:, :HD] / acc[:, HD:]).astype(jnp.bfloat16)
            if slot == 0:
                self_ref[:, pl.ds(pl.multiple_of(half * wide + h * HD, HD), HD)] = out
            else:
                st_so[:, cols] = out
            x = out.astype(jnp.float32)
            norm = lax.rsqrt(jnp.mean(x * x, axis=1, keepdims=True) + EPS)
            x = (x * norm).reshape(rows // 8, 8, HD) * gain_ref[...][None]
            x = x.reshape(rows, HD).astype(jnp.bfloat16)
            query_rows(slot, h, x.astype(jnp.float32))
            peak[slot, h] = jnp.full(peak.shape[2:], NEG, jnp.float32)
            mixed[slot, h] = jnp.zeros(mixed.shape[2:], jnp.float32)
        return 0

    def image_level(step):
        away = jnp.where(lax.rem(step, 2) == 0, step // 2, LEVELS - (step + 1) // 2)
        return lax.rem(z + away, LEVELS)

    def advance(step, _):
        @pl.when(step == 1)
        def _():
            forward(1, 2)

        @pl.when(step == 2)
        def _():
            forward(1, 3)
            lax.fori_loop(0, HEADS, finish_self, 0)
            x_so.start()

        @pl.when(step == 3)
        def _():
            forward(1, 4)

        @pl.when(step == 4)
        def _():
            forward(1, 5)

        @pl.when(step == 5)
        def _():
            forward(1, 6, (0,))

        @pl.when(step == 6)
        def _():
            forward(1, 6, (1,))

        level = image_level(jnp.maximum(step - 2, 0))
        text = jnp.where(step == 1, 1, jnp.where(z >= 6, 2 - early, 0))
        piece = jnp.where(step < 2, text, LEVELS // 2 + level)
        group = jnp.where(step < 2, 4, level // 2)

        @pl.when((step >= 2) | (z >= 2 + 2 * step))
        def _():
            load(piece)
            attend(both, group=group)
        return 0

    lax.fori_loop(0, 7, advance, 0)
    for d in (0, 1):
        await_in(1, d, 4)
        await_in(1, d, 5)

    def finish(turn, _):
        slot = 1 - turn
        tiles = [(slot, h) for h in range(HEADS)]

        def more(step, _):
            level = image_level(step)
            load(LEVELS // 2 + level)
            attend(tiles, group=level // 2)
            return 0

        lax.fori_loop(5, 7, more, 0)

        @pl.when(slot == 1)
        def _():
            x_so.wait_recv()
            self_ref[:, other_wide] = so_in[...]
            for d in (0, 1):
                await_in(1, d, 6)

        level = image_level(7)
        load(LEVELS // 2 + level)
        seen = seen_by(slot, level // 2)
        following = scores_of(tiles[0])
        for h, tile in enumerate(tiles):
            scores = following
            if h + 1 < HEADS:
                following = scores_of(tiles[h + 1])
            _, acc = fold(scores, held(tile), seen)
            gate = jnp.tanh(gate_ref[half * HEADS + h])[None]
            out = (acc[:, :HD] / jnp.maximum(acc[:, HD:], 1.0)).reshape(rows // 8, 8, HD) * gate
            st_co[slot, :, h * HD:(h + 1) * HD] = out.reshape(rows, HD).astype(jnp.bfloat16)
            if h % 2 == 1:
                @pl.when(slot == 1)
                def _():
                    x_co(h // 2).start()
        return 0

    lax.fori_loop(0, 2, finish, 0)
    cross_ref[:, own_wide] = st_co[0]
    for pair in range(HEADS // 2):
        x_co(pair).wait_recv()
    cross_ref[:, other_wide] = co_in[...]

    for copy in (x_self, x_query, x_allow, x_img, x_so):
        copy.wait_send()
    for pair in range(HEADS // 2):
        x_co(pair).wait_send()
    for kind in (0, 1):
        for d in (0, 1):
            for n in range(LAST + 1):
                outgoing(kind, d, n).wait_send()


def per_device(
    queries, keys, values, image_keys, image_values, cross_lo, cross_hi, query_gain, cross_gate
):
    rows, img_rows = queries.shape[0], image_keys.shape[0]
    wide = HEADS * HD
    first = jnp.arange(HD, dtype=jnp.int32)[None, :] * IMG
    allow = ((cross_lo[:, None] <= first) & (first < cross_hi[:, None])).astype(jnp.bfloat16)
    gate = jnp.broadcast_to(cross_gate[:, None, None], (cross_gate.shape[0], 8, HD))
    vmem = pl.BlockSpec(memory_space=pltpu.VMEM)
    bf16, f32 = jnp.bfloat16, jnp.float32
    return pl.pallas_call(
        kernel,
        out_shape=(jax.ShapeDtypeStruct(queries.shape, bf16),) * 2,
        in_specs=[vmem] * 8,
        out_specs=(vmem, vmem),
        scratch_shapes=[
            pltpu.VMEM((LEVELS // 2 + LEVELS, 4 * rows, 2 * HD), bf16),
            pltpu.VMEM((rows, 2 * HD), bf16),
            pltpu.VMEM((img_rows, 2 * HD), bf16),
            pltpu.VMEM((rows, wide), bf16),
            pltpu.VMEM((rows, HD), bf16),
            pltpu.VMEM((2, HEADS, rows, 2 * HD), bf16),
            pltpu.VMEM((2, HEADS, rows, HD), f32),
            pltpu.VMEM((2, HEADS, rows, 2 * HD), f32),
            pltpu.VMEM((2, 5, rows, HD), f32),
            pltpu.VMEM((rows, wide), bf16),
            pltpu.VMEM((2, rows, wide), bf16),
            pltpu.VMEM((rows, wide), bf16),
            pltpu.VMEM((rows, wide), bf16),
            pltpu.VMEM((4 * rows, 2 * HD), bf16),
            pltpu.VMEM((4 * rows, 2 * HD), bf16),
            pltpu.SemaphoreType.DMA((2, 2, LAST + 1)),
            pltpu.SemaphoreType.DMA((2, 2, LAST + 1)),
            pltpu.SemaphoreType.DMA((9,)),
            pltpu.SemaphoreType.DMA((9,)),
        ],
        compiler_params=pltpu.CompilerParams(
            collective_id=0, has_side_effects=True, vmem_limit_bytes=56 * 2**20
        ),
    )(queries, keys, values, image_keys, image_values, allow, jnp.broadcast_to(query_gain, (8, HD)), gate)


def solution(mesh):
    split = P(("doc", "ctx"), "head")
    return jax.shard_map(
        per_device,
        mesh=mesh,
        in_specs=(split,) * 5 + (P(("doc", "ctx")), P(("doc", "ctx")), P(), P("head")),
        out_specs=(split, split),
        check_vma=False,
    )
```

time: 554 us -> 109 us (0.20)
  the two profiles are of different devices: /device:TPU:118 before, /device:TPU:16 now
where the time goes in v1:
time: 109 us
  Pallas kernels  102 us (94%)
  local copies, waits for them, and re-layouts  5.42 us (5%)
    pallas_call x1, Pallas kernels, per_device(): pl.pallas_call(kernel, out_shape=(jax.ShapeDtypeStruct(queries.shape, bf1...  102 us
    unnamed x12, local copies, waits for them, and re-layouts  4.11 us

profile of v1, /device:TPU:16, one launch (start us, length us, event | category | flops | bytes accessed | tf_op | source)
XLA Modules:
  0.0 108.6 jit_solution(3285436241944826301)
XLA Ops:
  0.6 0.0 copy-start.4
  0.6 0.6 copy-done.4
  1.3 0.0 copy-start.1
  1.3 0.0 copy-start.2
  1.3 0.6 broadcast_in_dim.4.gain_ref
  1.9 0.1 copy-done.1
  2.0 0.0 copy-done.2
  2.0 0.0 copy-start.3
  2.0 0.8 and_convert_fusion.allow_ref
  2.8 0.0 copy-done.3
  2.8 0.7 broadcast_in_dim.5.gate_ref
  3.5 101.7 %shard_map.104 = (bf16[256,2048]{1,0:T(8,128)(2,1)}, bf16[256,2048]{1,0:T(8,128)(2,1)}) custom-call(bf16[256,2048]{1,0:T(8,128)(2,1)} %q_ref.1, bf16[256,256]{1,0:T(8,128)(2,1)} %k_ref.1, bf16[256,256]{1,0:T(8,128)(2,1)} %v_ref.1, bf16[512,256]{1,0:T(8,128)(2,1)} %ik_ref.1, bf16[512,256]{1,0:T(8,128)(2,1)} %iv_ref.1, ...), custom_call_target="tpu_custom_call" | custom-call | tf_op jit(solution)/shard_map/pallas_call | solution.py:379
  105.2 0.0 copy-start
  105.2 2.4 %copy.13 = bf16[256,2048]{1,0:T(8,128)(2,1)} copy(bf16[256,2048]{1,0:T(8,128)(2,1)} %get-tuple-element.4) | data formatting | bytes 2097152
  107.6 0.0 copy-done
  107.6 1.0 copy.14
  (1 shorter events, 0.0 us)
Async XLA Ops:
  0.6 0.7 copy-start.4
  1.3 0.7 copy-start.1
  1.3 0.7 copy-start.2
  2.0 0.8 copy-start.3
  105.2 2.4 %copy-start = (bf16[256,2048]{1,0:T(8,128)(2,1)S(1)}, bf16[256,2048]{1,0:T(8,128)(2,1)}, u32[]{:S(2)}) copy-start(bf16[256,2048]{1,0:T(8,128)(2,1)} %get-tuple-element.5) | copy-start | bytes 3145732

commit v2 on v1

--- a/solution.py
+++ b/solution.py
@@ -34,16 +34,17 @@
 
 
 def kernel(
-    q_ref, k_ref, v_ref, ik_ref, iv_ref, allow_ref, gain_ref, gate_ref,
+    q_hbm, k_hbm, v_hbm, ik_hbm, iv_hbm, low_hbm, high_hbm, gain_hbm, gate_hbm,
     self_ref, cross_ref,
     kv, st_self, st_img, q_in, allow_in, split_q, peak, mixed, allowed,
-    st_so, st_co, so_in, co_in, keys2, values1,
-    z_send, z_recv, x_send, x_recv,
+    st_so, st_co, so_in, co_in, keys2, values1, allow_ref,
+    q_own, q_out, low_ref, high_ref, gain_ref, gate_ref,
+    load_sem, z_send, z_recv, x_send, x_recv,
 ):
     me = lax.axis_index("ctx")
     z, half = me // 2, me % 2
-    rows = q_ref.shape[0]
-    img_rows = ik_ref.shape[0]
+    rows = q_hbm.shape[0]
+    img_rows = ik_hbm.shape[0]
     wide = HEADS * HD
     partner = {"ctx": z * 2 + (1 - half)}
     up = {"ctx": lax.rem(z + 1, LEVELS) * 2 + half}
@@ -65,15 +66,27 @@
         start = h * img_rows
         return kv.at[LEVELS // 2 + level, pl.ds(pl.multiple_of(start, img_rows), img_rows), :]
 
-    for kind, stage, key_ref, value_ref in (
-        (0, st_self, k_ref, v_ref),
-        (1, st_img, ik_ref, iv_ref),
+    fetches = []
+
+    def fetch(src, dst):
+        copy = pltpu.make_async_copy(src, dst, load_sem.at[len(fetches)])
+        fetches.append(copy)
+        copy.start()
+
+    for kind, stage, key_hbm, value_hbm in (
+        (0, st_self, k_hbm, v_hbm),
+        (1, st_img, ik_hbm, iv_hbm),
     ):
         mine = part(kind, z, half)
-        mine[:, :HD] = key_ref[:, own_col]
-        mine[:, HD:] = value_ref[:, own_col]
-        stage[:, :HD] = key_ref[:, other_col]
-        stage[:, HD:] = value_ref[:, other_col]
+        fetch(key_hbm.at[:, own_col], mine.at[:, pl.ds(0, HD)])
+        fetch(value_hbm.at[:, own_col], mine.at[:, pl.ds(HD, HD)])
+        fetch(key_hbm.at[:, other_col], stage.at[:, pl.ds(0, HD)])
+        fetch(value_hbm.at[:, other_col], stage.at[:, pl.ds(HD, HD)])
+        if kind == 0:
+            fetch(q_hbm.at[:, own_wide], q_own)
+            fetch(q_hbm.at[:, other_wide], q_out)
+    for src, dst in ((low_hbm, low_ref), (high_hbm, high_ref), (gain_hbm, gain_ref), (gate_hbm, gate_ref)):
+        fetch(src, dst)
 
     def x_copy(slot, src, dst):
         return pltpu.make_async_remote_copy(
@@ -82,7 +95,7 @@
         )
 
     x_self = x_copy(0, st_self, part(0, z, half))
-    x_query = x_copy(1, q_ref.at[:, other_wide], q_in)
+    x_query = x_copy(1, q_out, q_in)
     x_allow = x_copy(2, allow_ref, allow_in)
     x_img = x_copy(3, st_img, part(1, z, half))
     x_so = x_copy(4, st_so, so_in)
@@ -194,13 +207,28 @@
 
     values1[:, HD:] = jnp.ones((4 * rows, HD), jnp.bfloat16)
 
+    for copy in fetches[:4]:
+        copy.wait()
     pl.semaphore_wait(barrier, 3)
     x_self.start()
     forward(0, 0)
-    prepare(0, lambda cols: q_ref[:, pl.ds(pl.multiple_of(half * wide + cols.start, HD), HD)])
+    for copy in fetches[4:]:
+        copy.wait()
+    prepare(0, lambda cols: q_own[:, cols])
     x_self.wait_recv()
     x_query.start()
     forward(0, 1)
+    lane = lax.broadcasted_iota(jnp.int32, (HD, HD), 1)
+    diagonal = lane == lax.broadcasted_iota(jnp.int32, (HD, HD), 0)
+
+    def column(ref, block):
+        wide_row = jnp.broadcast_to(ref[block:block + 1, :].astype(jnp.float32), (HD, HD))
+        return jnp.sum(jnp.where(diagonal, wide_row, 0.0), axis=1, keepdims=True)
+
+    begins = (lane * IMG).astype(jnp.float32)
+    for block in range(rows // HD):
+        inside = (column(low_ref, block) <= begins) & (begins < column(high_ref, block))
+        allow_ref[block * HD:(block + 1) * HD, :] = jnp.where(inside, 1.0, 0.0).astype(jnp.bfloat16)
     forward(0, 2)
     forward(0, 3)
 
@@ -223,23 +251,32 @@
             forward(0, 4)
             forward(0, 5)
 
-        @pl.when(z >= 6)
-        def _():
-            load(early)
-            attend(tiles)
-
-        @pl.when(slot == 0)
-        def _():
-            forward(0, 6)
-            forward(1, 0)
+        def more(step, _):
+            @pl.when((slot == 0) & (step == 1))
+            def _():
+                forward(0, 6)
+                forward(1, 0)
+                for d in (0, 1):
+                    await_in(0, d, 4)
+                    await_in(0, d, 5)
+
+            @pl.when((slot == 1) & (step == 1))
+            def _():
+                x_img.wait_recv()
+                forward(1, 1)
+
+            @pl.when(z >= 6)
+            def _():
+                load(jnp.where(step == 0, early, 2 - early))
+                attend(tiles)
+            return 0
+
+        lax.fori_loop(0, 2, more, 0)
         return 0
 
     lax.fori_loop(0, 2, begin, 0)
-    x_img.wait_recv()
-    forward(1, 1)
     for d in (0, 1):
-        for n in (4, 5, 6):
-            await_in(0, d, n)
+        await_in(0, d, 6)
     x_allow.wait_recv()
     for slot, ref in ((0, allow_ref), (1, allow_in)):
         for image in range(4):
@@ -248,9 +285,9 @@
             )
         allowed[slot, 4] = jnp.ones(allowed.shape[2:], jnp.float32)
 
-    def finish_self(h, _):
-        cols = pl.ds(pl.multiple_of(h * HD, HD), HD)
-        for slot in (1, 0):
+    def finish_self(pair, _):
+        for slot, h in ((s, pair * 2 + u) for u in (0, 1) for s in (1, 0)):
+            cols = pl.ds(pl.multiple_of(h * HD, HD), HD)
             acc = mixed[slot, h]
             out = (acc[:, :HD] / acc[:, HD:]).astype(jnp.bfloat16)
             if slot == 0:
@@ -259,8 +296,7 @@
                 st_so[:, cols] = out
             x = out.astype(jnp.float32)
             norm = lax.rsqrt(jnp.mean(x * x, axis=1, keepdims=True) + EPS)
-            x = (x * norm).reshape(rows // 8, 8, HD) * gain_ref[...][None]
-            x = x.reshape(rows, HD).astype(jnp.bfloat16)
+            x = (x * norm * gain_ref[...]).astype(jnp.bfloat16)
             query_rows(slot, h, x.astype(jnp.float32))
             peak[slot, h] = jnp.full(peak.shape[2:], NEG, jnp.float32)
             mixed[slot, h] = jnp.zeros(mixed.shape[2:], jnp.float32)
@@ -271,15 +307,12 @@
         return lax.rem(z + away, LEVELS)
 
     def advance(step, _):
-        @pl.when(step == 1)
+        @pl.when(step == 2)
         def _():
             forward(1, 2)
-
-        @pl.when(step == 2)
-        def _():
+            lax.fori_loop(0, HEADS // 2, finish_self, 0)
+            x_so.start()
             forward(1, 3)
-            lax.fori_loop(0, HEADS, finish_self, 0)
-            x_so.start()
 
         @pl.when(step == 3)
         def _():
@@ -298,11 +331,11 @@
             forward(1, 6, (1,))
 
         level = image_level(jnp.maximum(step - 2, 0))
-        text = jnp.where(step == 1, 1, jnp.where(z >= 6, 2 - early, 0))
+        text = jnp.where(step == 1, 1, 0)
         piece = jnp.where(step < 2, text, LEVELS // 2 + level)
         group = jnp.where(step < 2, 4, level // 2)
 
-        @pl.when((step >= 2) | (z >= 2 + 2 * step))
+        @pl.when((step >= 2) | ((z >= 2 + 2 * step) & ((step == 1) | (z < 6))))
         def _():
             load(piece)
             attend(both, group=group)
@@ -312,6 +345,8 @@
     for d in (0, 1):
         await_in(1, d, 4)
         await_in(1, d, 5)
+
+    gate_lane = lax.broadcasted_iota(jnp.int32, gate_ref.shape, 1)
 
     def finish(turn, _):
         slot = 1 - turn
@@ -341,9 +376,11 @@
             if h + 1 < HEADS:
                 following = scores_of(tiles[h + 1])
             _, acc = fold(scores, held(tile), seen)
-            gate = jnp.tanh(gate_ref[half * HEADS + h])[None]
-            out = (acc[:, :HD] / jnp.maximum(acc[:, HD:], 1.0)).reshape(rows // 8, 8, HD) * gate
-            st_co[slot, :, h * HD:(h + 1) * HD] = out.reshape(rows, HD).astype(jnp.bfloat16)
+            gate = jnp.tanh(jnp.sum(
+                jnp.where(gate_lane == half * HEADS + h, gate_ref[...], 0.0), axis=1, keepdims=True
+            ))
+            out = acc[:, :HD] / jnp.maximum(acc[:, HD:], 1.0) * gate
+            st_co[slot, :, h * HD:(h + 1) * HD] = out.astype(jnp.bfloat16)
             if h % 2 == 1:
                 @pl.when(slot == 1)
                 def _():
@@ -371,15 +408,13 @@
 ):
     rows, img_rows = queries.shape[0], image_keys.shape[0]
     wide = HEADS * HD
-    first = jnp.arange(HD, dtype=jnp.int32)[None, :] * IMG
-    allow = ((cross_lo[:, None] <= first) & (first < cross_hi[:, None])).astype(jnp.bfloat16)
-    gate = jnp.broadcast_to(cross_gate[:, None, None], (cross_gate.shape[0], 8, HD))
     vmem = pl.BlockSpec(memory_space=pltpu.VMEM)
     bf16, f32 = jnp.bfloat16, jnp.float32
+    pin = lambda x: pltpu.with_memory_space_constraint(x, pltpu.HBM)
     return pl.pallas_call(
         kernel,
         out_shape=(jax.ShapeDtypeStruct(queries.shape, bf16),) * 2,
-        in_specs=[vmem] * 8,
+        in_specs=[pl.BlockSpec(memory_space=pltpu.HBM)] * 9,
         out_specs=(vmem, vmem),
         scratch_shapes=[
             pltpu.VMEM((LEVELS // 2 + LEVELS, 4 * rows, 2 * HD), bf16),
@@ -397,15 +432,27 @@
             pltpu.VMEM((rows, wide), bf16),
             pltpu.VMEM((4 * rows, 2 * HD), bf16),
             pltpu.VMEM((4 * rows, 2 * HD), bf16),
+            pltpu.VMEM((rows, HD), bf16),
+            pltpu.VMEM((rows, wide), bf16),
+            pltpu.VMEM((rows, wide), bf16),
+            pltpu.VMEM((rows // HD, HD), jnp.int32),
+            pltpu.VMEM((rows // HD, HD), jnp.int32),
+            pltpu.VMEM((1, HD), f32),
+            pltpu.VMEM((1, cross_gate.shape[0]), f32),
+            pltpu.SemaphoreType.DMA((14,)),
             pltpu.SemaphoreType.DMA((2, 2, LAST + 1)),
             pltpu.SemaphoreType.DMA((2, 2, LAST + 1)),
             pltpu.SemaphoreType.DMA((9,)),
             pltpu.SemaphoreType.DMA((9,)),
         ],
         compiler_params=pltpu.CompilerParams(
-            collective_id=0, has_side_effects=True, vmem_limit_bytes=56 * 2**20
+            collective_id=0, has_side_effects=True, vmem_limit_bytes=40 * 2**20
         ),
-    )(queries, keys, values, image_keys, image_values, allow, jnp.broadcast_to(query_gain, (8, HD)), gate)
+    )(
+        *(pin(x) for x in (queries, keys, values, image_keys, image_values)),
+        pin(cross_lo.reshape(-1, HD)), pin(cross_hi.reshape(-1, HD)), pin(query_gain[None, :]),
+        pin(cross_gate[None, :]),
+    )
 
 
 def solution(mesh):

time: 109 us -> 107 us (0.982)
  local copies, waits for them, and re-layouts: 5.42 us -> 1.94 us
  Pallas kernels: 102 us -> 104 us
    pallas_call x1, Pallas kernels: 102 us -> 104 us  [per_device(): pl.pallas_call(kernel, out_shape=(jax.ShapeDtypeStruct(queries.shape, bf1...]
    unnamed x12 -> x2, local copies, waits for them, and re-layouts: 4.11 us -> 1.94 us
    broadcast_in_dim x2 -> x0, local copies, waits for them, and re-layouts: 1.31 us -> none  [the longest x1 0.71 us: per_device(): jnp.broadcast_to(cross_gate[:, None, None], (cross_gate.shape[0], 8, HD))]
where the time goes in v2:
time: 107 us
  Pallas kernels  104 us (97%)
  local copies, waits for them, and re-layouts  1.94 us (2%)
    pallas_call x1, Pallas kernels, per_device(): pl.pallas_call(kernel, out_shape=(jax.ShapeDtypeStruct(queries.shape, bf1...  104 us

profile of v2, /device:TPU:16, one launch (start us, length us, event | category | flops | bytes accessed | tf_op | source)
XLA Modules:
  0.0 106.6 jit_solution(7049212923838497901)
XLA Ops:
  0.6 104.0 %shard_map.104 = (bf16[256,2048]{1,0:T(8,128)(2,1)S(1)}, bf16[256,2048]{1,0:T(8,128)(2,1)S(1)}) custom-call(bf16[256,2048]{1,0:T(8,128)(2,1)} %q_hbm.1, bf16[256,256]{1,0:T(8,128)(2,1)} %k_hbm.1, bf16[256,256]{1,0:T(8,128)(2,1)} %v_hbm.1, bf16[512,256]{1,0:T(8,128)(2,1)} %ik_hbm.1, bf16[512,256]{1,0:T(8,128)(2,1)} %iv_hbm.1, s32[2,128]{1,0:T(2,128)} %bitcast.4, ...), custom_call_target="tpu_custom_call" | custom-call | tf_op jit(solution)/shard_map/pallas_call | solution.py:414
  104.6 1.0 copy.13
  105.6 1.0 copy.14

commit v3 on v2

--- a/solution.py
+++ b/solution.py
@@ -185,12 +185,14 @@
     def own_order(slot):
         return lax.rem(half + slot, 2)
 
-    def attend(tiles, first=False, mask=None, group=None):
+    def attend(tiles, first=False, mask=None, group=None, before=lambda tile: None):
+        before(tiles[0])
         following = scores_of(tiles[0], mask)
         views = {}
         for n, tile in enumerate(tiles):
             scores = following
             if n + 1 < len(tiles):
+                before(tiles[n + 1])
                 following = scores_of(tiles[n + 1], mask)
             if group is not None and id(tile[0]) not in views:
                 views[id(tile[0])] = seen_by(tile[0], group)
@@ -285,34 +287,34 @@
             )
         allowed[slot, 4] = jnp.ones(allowed.shape[2:], jnp.float32)
 
-    def finish_self(pair, _):
-        for slot, h in ((s, pair * 2 + u) for u in (0, 1) for s in (1, 0)):
-            cols = pl.ds(pl.multiple_of(h * HD, HD), HD)
-            acc = mixed[slot, h]
-            out = (acc[:, :HD] / acc[:, HD:]).astype(jnp.bfloat16)
-            if slot == 0:
-                self_ref[:, pl.ds(pl.multiple_of(half * wide + h * HD, HD), HD)] = out
-            else:
-                st_so[:, cols] = out
-            x = out.astype(jnp.float32)
-            norm = lax.rsqrt(jnp.mean(x * x, axis=1, keepdims=True) + EPS)
-            x = (x * norm * gain_ref[...]).astype(jnp.bfloat16)
-            query_rows(slot, h, x.astype(jnp.float32))
-            peak[slot, h] = jnp.full(peak.shape[2:], NEG, jnp.float32)
-            mixed[slot, h] = jnp.zeros(mixed.shape[2:], jnp.float32)
-        return 0
+    def finish_self(tile):
+        slot, h = tile
+        acc = mixed[tile]
+        out = (acc[:, :HD] / acc[:, HD:]).astype(jnp.bfloat16)
+        if slot == 0:
+            self_ref[:, pl.ds(pl.multiple_of(half * wide + h * HD, HD), HD)] = out
+        else:
+            st_so[:, h * HD:(h + 1) * HD] = out
+        x = out.astype(jnp.float32)
+        norm = lax.rsqrt(jnp.mean(x * x, axis=1, keepdims=True) + EPS)
+        x = (x * norm * gain_ref[...]).astype(jnp.bfloat16)
+        query_rows(slot, h, x.astype(jnp.float32))
 
     def image_level(step):
         away = jnp.where(lax.rem(step, 2) == 0, step // 2, LEVELS - (step + 1) // 2)
         return lax.rem(z + away, LEVELS)
 
     def advance(step, _):
+        @pl.when(step == 1)
+        def _():
+            forward(1, 2)
+
         @pl.when(step == 2)
         def _():
-            forward(1, 2)
-            lax.fori_loop(0, HEADS // 2, finish_self, 0)
+            forward(1, 3)
+            load(LEVELS // 2 + z)
+            attend(both, True, group=z // 2, before=finish_self)
             x_so.start()
-            forward(1, 3)
 
         @pl.when(step == 3)
         def _():
@@ -326,7 +328,7 @@
         def _():
             forward(1, 6, (0,))
 
-        @pl.when(step == 6)
+        @pl.when(step == jnp.where(z >= 4, 5, 6))
         def _():
             forward(1, 6, (1,))
 
@@ -335,7 +337,7 @@
         piece = jnp.where(step < 2, text, LEVELS // 2 + level)
         group = jnp.where(step < 2, 4, level // 2)
 
-        @pl.when((step >= 2) | ((z >= 2 + 2 * step) & ((step == 1) | (z < 6))))
+        @pl.when((step >= 3) | ((step < 2) & (z >= 2 + 2 * step) & ((step == 1) | (z < 6))))
         def _():
             load(piece)
             attend(both, group=group)

time: 107 us -> 103 us (0.963)
  Pallas kernels: 104 us -> 101 us
    pallas_call x1, Pallas kernels: 104 us -> 101 us  [per_device(): pl.pallas_call(kernel, out_shape=(jax.ShapeDtypeStruct(queries.shape, bf1...]
where the time goes in v3:
time: 103 us
  Pallas kernels  101 us (98%)
  local copies, waits for them, and re-layouts  1.94 us (2%)
    pallas_call x1, Pallas kernels, per_device(): pl.pallas_call(kernel, out_shape=(jax.ShapeDtypeStruct(queries.shape, bf1...  101 us

profile of v3, /device:TPU:16, one launch (start us, length us, event | category | flops | bytes accessed | tf_op | source)
XLA Modules:
  0.0 103.3 jit_solution(7833124875287568300)
XLA Ops:
  0.6 100.7 %shard_map.104 = (bf16[256,2048]{1,0:T(8,128)(2,1)S(1)}, bf16[256,2048]{1,0:T(8,128)(2,1)S(1)}) custom-call(bf16[256,2048]{1,0:T(8,128)(2,1)} %q_hbm.1, bf16[256,256]{1,0:T(8,128)(2,1)} %k_hbm.1, bf16[256,256]{1,0:T(8,128)(2,1)} %v_hbm.1, bf16[512,256]{1,0:T(8,128)(2,1)} %ik_hbm.1, bf16[512,256]{1,0:T(8,128)(2,1)} %iv_hbm.1, s32[2,128]{1,0:T(2,128)} %bitcast.4, ...), custom_call_target="tpu_custom_call" | custom-call | tf_op jit(solution)/shard_map/pallas_call | solution.py:416
  101.3 1.0 copy.13
  102.3 1.0 copy.14
